TPU v7x, 32 devices: a whole 2x2x4 slice. The times are simulated.
32 devices in a mesh: ka: 16 (over z, y, core), ga: 2 (over x).
Axes of the slice: x: 2, y: 2, z: 4, core: 2. Of those that a mesh axis runs over, the one named last changes fastest.
Arguments:
- orbitals: bfloat16 [16, 16, 4096], P('ka', None, 'ga'), may hold values from -6 to 6
- interp_vectors: bfloat16 [4096, 4096], P(None, 'ga'), may hold values from -0.09375 to 0.09375
- screening: bfloat16 [9216, 4096], P('ka', 'ga'), may hold values from 0.049804688 to 2
- bare_coulomb: float32 [4096], P('ga'), may hold values from 0.05 to 2
- slab_kpoints: int32 [16], P('ka'), may hold values from 0 to 9215, as said below
Outputs:
- kernel: float32 [16, 7, 1, 4096], P('ka', None, None, 'ga')
Inputs may be any that keep to these rules, and one draw needn't show every extreme that they name: `slab_kpoints`: distinct grid points, each written as ix * 96 + iy with ix and iy its two grid coordinates.
All inputs are finite; a program needn't handle non-finite values.
Results may differ from a plain program's by a relative error of at most 0.0049.
Values may be sent and summed in bfloat16 or wider, within the bound.
A program may use at most 128 MiB of HBM per device.

v0:
```python
import jax
import jax.numpy as jnp
from jax import lax
from jax.sharding import PartitionSpec as P

NV = 8
NC = 8
NG = 4096
NKX = 96
RSTEPS = 3


def from_behind(block, axis, distance):
    devices = range(lax.axis_size(axis))
    route = [((i - distance) % len(devices), i) for i in devices]
    return lax.ppermute(block, axis, route)


def products_across(own_full, partner_full):
    product = (
        own_full.astype(jnp.float32)[:, None, :, None, :]
        * partner_full.astype(jnp.float32)[None, :, None, :, :]
    )
    return product.reshape(
        own_full.shape[0],
        partner_full.shape[0],
        own_full.shape[1] * partner_full.shape[1],
        own_full.shape[2],
    ).astype(jnp.bfloat16)


def project(points, interp_vectors):
    dims_in = points.shape
    flattened = points.reshape(-1, dims_in[-1])
    pair_waves = jnp.dot(flattened, interp_vectors, preferred_element_type=jnp.float32)
    return pair_waves.astype(jnp.bfloat16).reshape(dims_in[:-1] + (interp_vectors.shape[1],))


def exchange_of(block_full, interp_vectors):
    rows_here = block_full.shape[0]
    product = (
        block_full[:, :NV].astype(jnp.float32)[:, :, None, :]
        * block_full[:, NV:].astype(jnp.float32)[:, None, :, :]
    )
    return project(product.reshape(rows_here, NV * NC, -1).astype(jnp.bfloat16), interp_vectors)


def momentum_index(first_point, second_point):
    row_step = (first_point // NKX - second_point // NKX) % NKX
    col_step = (first_point % NKX - second_point % NKX) % NKX
    return row_step * NKX + col_step


def pair_block(own_full, partner_full, weighted_x, partner_ex, screen_rows, interp_vectors):
    rows_here = own_full.shape[0]
    cond_pairs = products_across(own_full[:, NV:], partner_full[:, NV:])
    vale_pairs = products_across(own_full[:, :NV], partner_full[:, :NV])
    pair_waves = project(jnp.concatenate([cond_pairs, vale_pairs], axis=2), interp_vectors)
    weighted = (
        pair_waves[:, :, : NC * NC].astype(jnp.float32) * screen_rows[:, :, None, :]
    ).astype(jnp.bfloat16)
    direct = jnp.einsum(
        "klxg,klyg->klxy", weighted, pair_waves[:, :, NC * NC :], preferred_element_type=jnp.float32
    )
    direct = (
        direct.reshape(rows_here, rows_here, NC, NC, NV, NV)
        .transpose(0, 1, 4, 2, 5, 3)
        .reshape(rows_here, rows_here, -1)
    )
    exch_term = jnp.einsum(
        "kxg,lyg->klxy", weighted_x, partner_ex, preferred_element_type=jnp.float32
    )
    return 2.0 * exch_term.reshape(rows_here, rows_here, -1) - direct


def per_device(orbitals, interp_vectors, screening, bare_coulomb, slab_kpoints):
    cycle_size = lax.axis_size("ka")
    own_full = lax.all_gather(orbitals, "ga", axis=2, tiled=True)
    own_exchange = exchange_of(own_full, interp_vectors)
    weighted_x = (own_exchange.astype(jnp.float32) * bare_coulomb).astype(jnp.bfloat16)
    offsets = list(range(-RSTEPS, RSTEPS + 1))
    momenta = []
    for offset in offsets:
        if offset == 0:
            partner = slab_kpoints
        else:
            partner = from_behind(slab_kpoints, "ka", offset)
        momenta.append(momentum_index(slab_kpoints[:, None], partner[None, :]))
    wanted = jnp.stack(momenta).reshape(-1)
    rows_here = slab_kpoints.shape[0]
    table_rows = screening.shape[0]
    owners = wanted // table_rows
    holders = jnp.arange(cycle_size, dtype=jnp.int32)[:, None]
    queries = jnp.where(owners[None, :] == holders, (wanted % table_rows)[None, :], -1)
    received = lax.all_to_all(queries, "ka", split_axis=0, concat_axis=0, tiled=True)
    picker = (
        received.reshape(-1)[:, None] == jnp.arange(table_rows, dtype=jnp.int32)[None, :]
    ).astype(jnp.bfloat16)
    replies = jnp.dot(picker, screening, preferred_element_type=jnp.float32).astype(jnp.bfloat16)
    replies = replies.reshape(cycle_size, wanted.shape[0], -1)
    returned = lax.all_to_all(replies, "ka", split_axis=0, concat_axis=0, tiled=True)
    fetched = jnp.sum(returned.astype(jnp.float32), axis=0)
    screen_rows = fetched.reshape(len(offsets), rows_here, rows_here, -1)
    partials = {
        0: pair_block(
            own_full, own_full, weighted_x, own_exchange, screen_rows[RSTEPS], interp_vectors
        )
    }
    forward_block = (own_full, own_exchange)
    backward_block = (own_full, own_exchange)
    for travel in range(1, RSTEPS + 1):
        forward_block = from_behind((forward_block[0], forward_block[1]), "ka", 1)
        backward_block = from_behind((backward_block[0], backward_block[1]), "ka", -1)
        partials[travel] = pair_block(
            own_full,
            forward_block[0],
            weighted_x,
            forward_block[1],
            screen_rows[RSTEPS + travel],
            interp_vectors,
        )
        partials[-travel] = pair_block(
            own_full,
            backward_block[0],
            weighted_x,
            backward_block[1],
            screen_rows[RSTEPS - travel],
            interp_vectors,
        )
    partial_terms = jnp.stack([partials[offset] for offset in offsets], axis=1)
    summed = lax.psum_scatter(partial_terms, "ga", scatter_dimension=3, tiled=True)
    return summed * NG ** (-0.5)


def solution(mesh):
    in_specs = (P("ka", None, "ga"), P(None, "ga"), P("ka", "ga"), P("ga"), P("ka"))
    out_specs = P("ka", None, None, "ga")
    return jax.shard_map(
        per_device, mesh=mesh, in_specs=in_specs, out_specs=out_specs, check_vma=False
    )
```

profile of v0, /device:TPU:0, one launch (start us, length us, event | category | flops | bytes accessed | tf_op | source)
XLA Modules:
  0.0 216.2 jit_solution(13168728564082243755)
XLA Ops:
  6.5 6.0 %collective-permute-start.7 = (s32[1]{0:T(128)}, s32[1]{0:T(128)}, u32[]{:S(2)}, u32[]{:S(2)}) collective-permute-start(s32[1]{0:T(128)} %param.9), channel_id=1, source_target_pairs={{4,0},{6,2},{8,4},{10,6},{12,8},{14,10},{16,12},{18,14},{20,16},{2... | collective-permute-start | bytes 20 | tf_op jit(solution)/shard_map/ppermute | solution.py:16
  12.5 1.6 collective-permute-start.8
  14.2 2.8 %collective-permute-start.11 = (s32[1]{0:T(128)}, s32[1]{0:T(128)}, u32[]{:S(2)}, u32[]{:S(2)}) collective-permute-start(s32[1]{0:T(128)} %param.9), channel_id=1, source_target_pairs={{26,0},{28,2},{30,4},{0,6},{2,8},{4,10},{6,12},{8,14},{10,16},{12,... | collective-permute-start | bytes 20 | tf_op jit(solution)/shard_map/ppermute | solution.py:16
  17.6 5.2 %all_gather.3 = bf16[1,16,4096]{2,1,0:T(8,128)(2,1)S(1)} all-gather(bf16[1,16,2048]{2,1,0:T(8,128)(2,1)} %param.5), channel_id=1, replica_groups=mesh['ka'=16,'ga'=2] {'ga'}, dimensions={2}, use_global_device_ids=true | all-gather | bytes 196608 | tf_op jit(solution)/shard_map/all_gather | solution.py:78
  22.9 8.8 %convolution_convert_fusion.8 = bf16[64,2048]{1,0:T(8,128)(2,1)S(1)} fusion(bf16[4096,2048]{1,0:T(8,128)(2,1)} %param.6, f32[8,4096]{1,0:T(8,128)S(1)} %get-tuple-element.32, f32[8,4096]{1,0:T(8,128)S(1)} %get-tuple-element.31), kind=kOutput, calls=%fused_computation.17 | convolution fusion | flops 1074397184 | bytes 17301504 | tf_op jit(solution)/shard_map/dot_general | solution.py:35
  33.7 1.9 collective-permute-start.3
  41.4 4.5 %collective-permute-start = (bf16[1,64,2048]{2,1,0:T(8,128)(2,1)S(1)}, bf16[1,64,2048]{2,1,0:T(8,128)(2,1)}, u32[]{:S(2)}, u32[]{:S(2)}) collective-permute-start(bf16[1,64,2048]{2,1,0:T(8,128)(2,1)S(1)} %bitcast.393), channel_id=1, source_target_pairs={{2,0},{4,2},{6,4},{8,6},{10,8},{12,10},{14,12},{16,14},{18,16},{20... | collective-permute-start | bytes 786440 | tf_op jit(solution)/shard_map/ppermute | solution.py:16
  50.4 3.5 %all-to-all-start = ((s32[16,1,7]{2,1,0:T(1,128)}), s32[16,1,7]{2,1,0:T(1,128)S(1)}, u32[]{:S(2)}, u32[]{:S(2)}) async-start(s32[16,1,7]{2,1,0:T(1,128)} %compare_select_fusion), calls=%async_computation | async-start | bytes 16384 | tf_op jit(solution)/shard_map/all_to_all | solution.py:95
  54.3 5.9 %all-to-all-done = s32[16,1,7]{2,1,0:T(1,128)S(1)} async-done(((s32[16,1,7]{2,1,0:T(1,128)}), s32[16,1,7]{2,1,0:T(1,128)S(1)}, u32[]{:S(2)}, u32[]{:S(2)}) %all-to-all-start) | async-done | bytes 480 | tf_op jit(solution)/shard_map/all_to_all | solution.py:95
  63.0 3.6 %all-to-all-start.1 = ((bf16[16,7,2048]{2,1,0:T(8,128)(2,1)}), bf16[16,7,2048]{2,1,0:T(8,128)(2,1)S(1)}, u32[]{:S(2)}, u32[]{:S(2)}) async-start(bf16[16,7,2048]{2,1,0:T(8,128)(2,1)} %reshape.1073), calls=%async_computation.1 | async-start | bytes 1048576 | tf_op jit(solution)/shard_map/all_to_all | solution.py:101
  67.8 4.2 %collective-permute-start.4 = (bf16[1,16,4096]{2,1,0:T(8,128)(2,1)}, bf16[1,16,4096]{2,1,0:T(8,128)(2,1)S(1)}, u32[]{:S(2)}, u32[]{:S(2)}) collective-permute-start(bf16[1,16,4096]{2,1,0:T(8,128)(2,1)} %collective-permute-done.3), channel_id=1, source_target_pairs={{2,0},{4,2},{6,4},{8,6},{10,8},{12,10},{14,12},{16,14},{18,16},{20... | collective-permute-start | bytes 393224 | tf_op jit(solution)/shard_map/ppermute | solution.py:16
  75.7 6.8 %collective-permute-done.15 = bf16[1,16,4096]{2,1,0:T(8,128)(2,1)S(1)} collective-permute-done((bf16[1,16,4096]{2,1,0:T(8,128)(2,1)}, bf16[1,16,4096]{2,1,0:T(8,128)(2,1)S(1)}, u32[]{:S(2)}, u32[]{:S(2)}) %collective-permute-start.15) | collective-permute-done | bytes 131104 | tf_op jit(solution)/shard_map/ppermute | solution.py:16
  82.5 4.5 %collective-permute-start.5 = (bf16[1,16,4096]{2,1,0:T(8,128)(2,1)S(1)}, bf16[1,16,4096]{2,1,0:T(8,128)(2,1)S(1)}, u32[]{:S(2)}, u32[]{:S(2)}) collective-permute-start(bf16[1,16,4096]{2,1,0:T(8,128)(2,1)S(1)} %collective-permute-done.4), channel_id=1, source_target_pairs={{2,0},{4,2},{6,4},{8,6},{10,8},{12,10},{14,12},{16,14},{18,16},{20... | collective-permute-start | bytes 393224 | tf_op jit(solution)/shard_map/ppermute | solution.py:16
  87.1 4.4 %collective-permute-start.1 = (bf16[1,64,2048]{2,1,0:T(8,128)(2,1)}, bf16[1,64,2048]{2,1,0:T(8,128)(2,1)}, u32[]{:S(2)}, u32[]{:S(2)}) collective-permute-start(bf16[1,64,2048]{2,1,0:T(8,128)(2,1)} %collective-permute-done), channel_id=1, source_target_pairs={{2,0},{4,2},{6,4},{8,6},{10,8},{12,10},{14,12},{16,14},{18,16},{20... | collective-permute-start | bytes 786440 | tf_op jit(solution)/shard_map/ppermute | solution.py:16
  91.6 1.5 fusion.42
  93.2 9.7 %fusion.6 = bf16[1,1,128,2048]{3,2,1,0:T(8,128)(2,1)} fusion(bf16[4096,2048]{1,0:T(8,128)(2,1)} %param.6, bf16[1,1,64,4096]{3,2,1,0:T(8,128)(2,1)S(1)} %get-tuple-element.48, bf16[1,1,64,4096]{3,2,1,0:T(8,128)(2,1)S(1)} %get-tuple-element.5), kind=kOutput, calls=%fused_computation.16 | convolution fusion | flops 2149842944 | bytes 18350080 | tf_op jit(solution)/shard_map/dot_general | solution.py:35
  102.9 3.3 %fusion.1 = bf16[1,1,128,2048]{3,2,1,0:T(8,128)(2,1)} fusion(bf16[4096,2048]{1,0:T(8,128)(2,1)S(1)} %bitcast.391, bf16[1,1,64,4096]{3,2,1,0:T(8,128)(2,1)S(1)} %get-tuple-element.46, bf16[1,1,64,4096]{3,2,1,0:T(8,128)(2,1)S(1)} %get-tuple-element.6), kind=kOutput, calls=%fused_computation.11 | convolution fusion | flops 2149842944 | bytes 18350080 | tf_op jit(solution)/shard_map/dot_general | solution.py:35
  106.2 3.3 %fusion.2 = bf16[1,1,128,2048]{3,2,1,0:T(8,128)(2,1)} fusion(bf16[4096,2048]{1,0:T(8,128)(2,1)S(1)} %bitcast.391, bf16[1,1,64,4096]{3,2,1,0:T(8,128)(2,1)S(1)} %get-tuple-element.45, bf16[1,1,64,4096]{3,2,1,0:T(8,128)(2,1)S(1)} %get-tuple-element.7), kind=kOutput, calls=%fused_computation.12 | convolution fusion | flops 2149842944 | bytes 18350080 | tf_op jit(solution)/shard_map/dot_general | solution.py:35
  109.5 3.3 %fusion.3 = bf16[1,1,128,2048]{3,2,1,0:T(8,128)(2,1)} fusion(bf16[4096,2048]{1,0:T(8,128)(2,1)S(1)} %bitcast.391, bf16[1,1,64,4096]{3,2,1,0:T(8,128)(2,1)S(1)} %get-tuple-element.42, bf16[1,1,64,4096]{3,2,1,0:T(8,128)(2,1)S(1)} %get-tuple-element.8), kind=kOutput, calls=%fused_computation.13 | convolution fusion | flops 2149842944 | bytes 18350080 | tf_op jit(solution)/shard_map/dot_general | solution.py:35
  112.8 3.5 %fusion.4 = bf16[1,1,128,2048]{3,2,1,0:T(8,128)(2,1)} fusion(bf16[4096,2048]{1,0:T(8,128)(2,1)S(1)} %bitcast.391, bf16[1,1,64,4096]{3,2,1,0:T(8,128)(2,1)S(1)} %get-tuple-element.44, bf16[1,1,64,4096]{3,2,1,0:T(8,128)(2,1)S(1)} %get-tuple-element.9), kind=kOutput, calls=%fused_computation.14 | convolution fusion | flops 2149842944 | bytes 18350080 | tf_op jit(solution)/shard_map/dot_general | solution.py:35
  116.3 2.5 %fusion.5 = bf16[1,1,128,2048]{3,2,1,0:T(8,128)(2,1)S(1)} fusion(bf16[4096,2048]{1,0:T(8,128)(2,1)S(1)} %bitcast.391, bf16[1,1,64,4096]{3,2,1,0:T(8,128)(2,1)S(1)} %get-tuple-element.43, bf16[1,1,64,4096]{3,2,1,0:T(8,128)(2,1)S(1)} %get-tuple-element.10), kind=kOutput, calls=%fused_computation.15 | convolution fusion | flops 2149842944 | bytes 18350080 | tf_op jit(solution)/shard_map/dot_general | solution.py:35
  118.8 2.5 %fusion = bf16[1,1,128,2048]{3,2,1,0:T(8,128)(2,1)S(1)} fusion(bf16[4096,2048]{1,0:T(8,128)(2,1)S(1)} %bitcast.391, bf16[1,1,64,4096]{3,2,1,0:T(8,128)(2,1)S(1)} %get-tuple-element.47, bf16[1,1,64,4096]{3,2,1,0:T(8,128)(2,1)S(1)} %get-tuple-element.11), kind=kOutput, calls=%fused_computation.10 | convolution fusion | flops 2149842944 | bytes 18350080 | tf_op jit(solution)/shard_map/dot_general | solution.py:35
  121.4 1.2 fusion.8
  122.9 4.4 %collective-permute-start.2 = (bf16[1,64,2048]{2,1,0:T(8,128)(2,1)}, bf16[1,64,2048]{2,1,0:T(8,128)(2,1)S(1)}, u32[]{:S(2)}, u32[]{:S(2)}) collective-permute-start(bf16[1,64,2048]{2,1,0:T(8,128)(2,1)} %collective-permute-done.1), channel_id=1, source_target_pairs={{2,0},{4,2},{6,4},{8,6},{10,8},{12,10},{14,12},{16,14},{18,16},{20... | collective-permute-start | bytes 786440 | tf_op jit(solution)/shard_map/ppermute | solution.py:16
  132.1 1.9 convolution_bitcast_fusion
  134.4 1.9 convolution_bitcast_fusion.5
  136.6 1.9 convolution_bitcast_fusion.4
  143.8 8.8 %copy.56 = f32[1,7,1,4096]{2,1,0,3:T(8,128)} copy(f32[1,7,1,4096]{3,2,1,0:T(1,128)S(1)} %constant_dynamic-update-slice_fusion) | data formatting | bytes 229376
  152.5 11.1 %bitcast_reduce_fusion = f32[4096,7]{1,0:T(8,128)} fusion(f32[1,7,1,4096]{2,1,0,3:T(8,128)} %copy.56), kind=kLoop, calls=%fused_computation | loop fusion | bytes 229376
  163.6 33.2 %reduce-scatter.4.cloned.1.call-done = f32[2048,7]{1,0:T(8,128)} async-done(((f32[4096,7]{1,0:T(8,128)}), f32[2048,7]{1,0:T(8,128)}) %reduce-scatter.4.cloned.1.call-update) | async-done | bytes 57360
  196.8 6.8 %reshape_bitcast_fusion = f32[1,7,1,2048]{2,1,0,3:T(8,128)} fusion(f32[2048,7]{1,0:T(8,128)} %reduce-scatter.4.cloned.1.call-done), kind=kLoop, calls=%fused_computation.1 | loop fusion | bytes 114688
  203.6 5.1 %copy.57 = f32[1,7,1,2048]{3,2,1,0:T(1,128)S(1)} copy(f32[1,7,1,2048]{2,1,0,3:T(8,128)} %reshape_bitcast_fusion) | data formatting | bytes 114688
  (115 shorter events, 20.6 us)
Async XLA Ops:
  6.5 54.9 %copy-start = (bf16[576,2048]{1,0:T(8,128)(2,1)S(1)}, bf16[576,2048]{1,0:T(8,128)(2,1)}, u32[]{:S(2)}) copy-start(bf16[576,2048]{1,0:T(8,128)(2,1)} %param.7) | copy-start | bytes 7077892
  6.5 25.1 %collective-permute-start.7 = (s32[1]{0:T(128)}, s32[1]{0:T(128)}, u32[]{:S(2)}, u32[]{:S(2)}) collective-permute-start(s32[1]{0:T(128)} %param.9), channel_id=1, source_target_pairs={{4,0},{6,2},{8,4},{10,6},{12,8},{14,10},{16,12},{18,14},{20,16},{2... | collective-permute-start | bytes 20 | tf_op jit(solution)/shard_map/ppermute | solution.py:16
  12.5 21.1 %collective-permute-start.6 = (s32[1]{0:T(128)}, s32[1]{0:T(128)}, u32[]{:S(2)}, u32[]{:S(2)}) collective-permute-start(s32[1]{0:T(128)} %param.9), channel_id=1, source_target_pairs={{6,0},{8,2},{10,4},{12,6},{14,8},{16,10},{18,12},{20,14},{22,16},{... | collective-permute-start | bytes 20 | tf_op jit(solution)/shard_map/ppermute | solution.py:16
  12.5 24.8 %collective-permute-start.8 = (s32[1]{0:T(128)}, s32[1]{0:T(128)}, u32[]{:S(2)}, u32[]{:S(2)}) collective-permute-start(s32[1]{0:T(128)} %param.9), channel_id=1, source_target_pairs={{2,0},{4,2},{6,4},{8,6},{10,8},{12,10},{14,12},{16,14},{18,16},{20... | collective-permute-start | bytes 20 | tf_op jit(solution)/shard_map/ppermute | solution.py:16
  14.2 25.2 %collective-permute-start.9 = (s32[1]{0:T(128)}, s32[1]{0:T(128)}, u32[]{:S(2)}, u32[]{:S(2)}) collective-permute-start(s32[1]{0:T(128)} %param.9), channel_id=1, source_target_pairs={{30,0},{0,2},{2,4},{4,6},{6,8},{8,10},{10,12},{12,14},{14,16},{16,... | collective-permute-start | bytes 20 | tf_op jit(solution)/shard_map/ppermute | solution.py:16
  14.2 27.2 %collective-permute-start.11 = (s32[1]{0:T(128)}, s32[1]{0:T(128)}, u32[]{:S(2)}, u32[]{:S(2)}) collective-permute-start(s32[1]{0:T(128)} %param.9), channel_id=1, source_target_pairs={{26,0},{28,2},{30,4},{0,6},{2,8},{4,10},{6,12},{8,14},{10,16},{12,... | collective-permute-start | bytes 20 | tf_op jit(solution)/shard_map/ppermute | solution.py:16
  22.8 31.0 %copy-start.4 = (f32[2048]{0:T(1024)S(1)}, f32[2048]{0:T(1024)}, u32[]{:S(2)}) copy-start(f32[2048]{0:T(1024)} %param.8) | copy-start | bytes 24580
  31.7 16.0 %collective-permute-start.10 = (s32[1]{0:T(128)}, s32[1]{0:T(128)}, u32[]{:S(2)}, u32[]{:S(2)}) collective-permute-start(s32[1]{0:T(128)} %param.9), channel_id=1, source_target_pairs={{28,0},{30,2},{0,4},{2,6},{4,8},{6,10},{8,12},{10,14},{12,16},{14,... | collective-permute-start | bytes 20 | tf_op jit(solution)/shard_map/ppermute | solution.py:16
  33.7 34.2 %collective-permute-start.3 = (bf16[1,16,4096]{2,1,0:T(8,128)(2,1)S(1)}, bf16[1,16,4096]{2,1,0:T(8,128)(2,1)}, u32[]{:S(2)}, u32[]{:S(2)}) collective-permute-start(bf16[1,16,4096]{2,1,0:T(8,128)(2,1)S(1)} %all_gather.3), channel_id=1, source_target_pairs={{2,0},{4,2},{6,4},{8,6},{10,8},{12,10},{14,12},{16,14},{18,16},{20... | collective-permute-start | bytes 393224 | tf_op jit(solution)/shard_map/ppermute | solution.py:16
  37.4 29.2 %collective-permute-start.13 = (bf16[1,16,4096]{2,1,0:T(8,128)(2,1)S(1)}, bf16[1,16,4096]{2,1,0:T(8,128)(2,1)}, u32[]{:S(2)}, u32[]{:S(2)}) collective-permute-start(bf16[1,16,4096]{2,1,0:T(8,128)(2,1)S(1)} %all_gather.3), channel_id=1, source_target_pairs={{30,0},{0,2},{2,4},{4,6},{6,8},{8,10},{10,12},{12,14},{14,16},{16,... | collective-permute-start | bytes 393224 | tf_op jit(solution)/shard_map/ppermute | solution.py:16
  39.4 33.6 %collective-permute-start.12 = (bf16[1,64,2048]{2,1,0:T(8,128)(2,1)S(1)}, bf16[1,64,2048]{2,1,0:T(8,128)(2,1)}, u32[]{:S(2)}, u32[]{:S(2)}) collective-permute-start(bf16[1,64,2048]{2,1,0:T(8,128)(2,1)S(1)} %bitcast.392), channel_id=1, source_target_pairs={{30,0},{0,2},{2,4},{4,6},{6,8},{8,10},{10,12},{12,14},{14,16},{16,... | collective-permute-start | bytes 786440 | tf_op jit(solution)/shard_map/ppermute | solution.py:16
  41.4 32.9 %collective-permute-start = (bf16[1,64,2048]{2,1,0:T(8,128)(2,1)S(1)}, bf16[1,64,2048]{2,1,0:T(8,128)(2,1)}, u32[]{:S(2)}, u32[]{:S(2)}) collective-permute-start(bf16[1,64,2048]{2,1,0:T(8,128)(2,1)S(1)} %bitcast.393), channel_id=1, source_target_pairs={{2,0},{4,2},{6,4},{8,6},{10,8},{12,10},{14,12},{16,14},{18,16},{20... | collective-permute-start | bytes 786440 | tf_op jit(solution)/shard_map/ppermute | solution.py:16
  50.4 9.8 %all-to-all-start = ((s32[16,1,7]{2,1,0:T(1,128)}), s32[16,1,7]{2,1,0:T(1,128)S(1)}, u32[]{:S(2)}, u32[]{:S(2)}) async-start(s32[16,1,7]{2,1,0:T(1,128)} %compare_select_fusion), calls=%async_computation | async-start | bytes 16384 | tf_op jit(solution)/shard_map/all_to_all | solution.py:95
  63.0 69.0 %all-to-all-start.1 = ((bf16[16,7,2048]{2,1,0:T(8,128)(2,1)}), bf16[16,7,2048]{2,1,0:T(8,128)(2,1)S(1)}, u32[]{:S(2)}, u32[]{:S(2)}) async-start(bf16[16,7,2048]{2,1,0:T(8,128)(2,1)} %reshape.1073), calls=%async_computation.1 | async-start | bytes 1048576 | tf_op jit(solution)/shard_map/all_to_all | solution.py:101
  66.5 130.3 %reduce-scatter.4.cloned.1.call-start = ((), (), s32[]{:S(2)}) async-start(), calls=%async_computation.3 | async-start | bytes 3145728
  66.6 15.9 %collective-permute-start.15 = (bf16[1,16,4096]{2,1,0:T(8,128)(2,1)}, bf16[1,16,4096]{2,1,0:T(8,128)(2,1)S(1)}, u32[]{:S(2)}, u32[]{:S(2)}) collective-permute-start(bf16[1,16,4096]{2,1,0:T(8,128)(2,1)} %collective-permute-done.13), channel_id=1, source_target_pairs={{30,0},{0,2},{2,4},{4,6},{6,8},{8,10},{10,12},{12,14},{14,16},{16,... | collective-permute-start | bytes 393224 | tf_op jit(solution)/shard_map/ppermute | solution.py:16
  67.8 14.7 %collective-permute-start.4 = (bf16[1,16,4096]{2,1,0:T(8,128)(2,1)}, bf16[1,16,4096]{2,1,0:T(8,128)(2,1)S(1)}, u32[]{:S(2)}, u32[]{:S(2)}) collective-permute-start(bf16[1,16,4096]{2,1,0:T(8,128)(2,1)} %collective-permute-done.3), channel_id=1, source_target_pairs={{2,0},{4,2},{6,4},{8,6},{10,8},{12,10},{14,12},{16,14},{18,16},{20... | collective-permute-start | bytes 393224 | tf_op jit(solution)/shard_map/ppermute | solution.py:16
  82.5 9.1 %collective-permute-start.17 = (bf16[1,16,4096]{2,1,0:T(8,128)(2,1)S(1)}, bf16[1,16,4096]{2,1,0:T(8,128)(2,1)S(1)}, u32[]{:S(2)}, u32[]{:S(2)}) collective-permute-start(bf16[1,16,4096]{2,1,0:T(8,128)(2,1)S(1)} %collective-permute-done.15), channel_id=1, source_target_pairs={{30,0},{0,2},{2,4},{4,6},{6,8},{8,10},{10,12},{12,14},{14,16},{16,... | collective-permute-start | bytes 393224 | tf_op jit(solution)/shard_map/ppermute | solution.py:16
  82.5 9.0 %collective-permute-start.5 = (bf16[1,16,4096]{2,1,0:T(8,128)(2,1)S(1)}, bf16[1,16,4096]{2,1,0:T(8,128)(2,1)S(1)}, u32[]{:S(2)}, u32[]{:S(2)}) collective-permute-start(bf16[1,16,4096]{2,1,0:T(8,128)(2,1)S(1)} %collective-permute-done.4), channel_id=1, source_target_pairs={{2,0},{4,2},{6,4},{8,6},{10,8},{12,10},{14,12},{16,14},{18,16},{20... | collective-permute-start | bytes 393224 | tf_op jit(solution)/shard_map/ppermute | solution.py:16
  87.0 34.4 %collective-permute-start.14 = (bf16[1,64,2048]{2,1,0:T(8,128)(2,1)}, bf16[1,64,2048]{2,1,0:T(8,128)(2,1)}, u32[]{:S(2)}, u32[]{:S(2)}) collective-permute-start(bf16[1,64,2048]{2,1,0:T(8,128)(2,1)} %collective-permute-done.12), channel_id=1, source_target_pairs={{30,0},{0,2},{2,4},{4,6},{6,8},{8,10},{10,12},{12,14},{14,16},{16,... | collective-permute-start | bytes 786440 | tf_op jit(solution)/shard_map/ppermute | solution.py:16
  87.1 35.8 %collective-permute-start.1 = (bf16[1,64,2048]{2,1,0:T(8,128)(2,1)}, bf16[1,64,2048]{2,1,0:T(8,128)(2,1)}, u32[]{:S(2)}, u32[]{:S(2)}) collective-permute-start(bf16[1,64,2048]{2,1,0:T(8,128)(2,1)} %collective-permute-done), channel_id=1, source_target_pairs={{2,0},{4,2},{6,4},{8,6},{10,8},{12,10},{14,12},{16,14},{18,16},{20... | collective-permute-start | bytes 786440 | tf_op jit(solution)/shard_map/ppermute | solution.py:16
  91.6 11.3 %slice-start = ((s8[16777216]{0:T(1024)(128)(4,1)}), s8[4194304]{0:T(1024)(128)(4,1)S(1)}, s32[]{:S(2)}) async-start(s8[16777216]{0:T(1024)(128)(4,1)} %bitcast.390), calls=%async_computation.4 | async-start | bytes 8388608
  91.6 11.3 %slice-start.1 = ((s8[16777216]{0:T(1024)(128)(4,1)}), s8[4194304]{0:T(1024)(128)(4,1)S(1)}, s32[]{:S(2)}) async-start(s8[16777216]{0:T(1024)(128)(4,1)} %bitcast.390), calls=%async_computation.5 | async-start | bytes 8388608
  93.1 9.7 %slice-start.2 = ((s8[16777216]{0:T(1024)(128)(4,1)}), s8[4194304]{0:T(1024)(128)(4,1)S(1)}, s32[]{:S(2)}) async-start(s8[16777216]{0:T(1024)(128)(4,1)} %bitcast.390), calls=%async_computation.6 | async-start | bytes 8388608
  93.2 9.7 %slice-start.3 = ((s8[16777216]{0:T(1024)(128)(4,1)}), s8[4194304]{0:T(1024)(128)(4,1)S(1)}, s32[]{:S(2)}) async-start(s8[16777216]{0:T(1024)(128)(4,1)} %bitcast.390), calls=%async_computation.7 | async-start | bytes 8388608
  121.4 17.4 %copy-start.3 = (bf16[1,1,128,2048]{3,2,1,0:T(8,128)(2,1)S(1)}, bf16[1,1,128,2048]{3,2,1,0:T(8,128)(2,1)}, u32[]{:S(2)}) copy-start(bf16[1,1,128,2048]{3,2,1,0:T(8,128)(2,1)} %fusion.3) | copy-start | bytes 1572868
  121.4 18.6 %copy-start.2 = (bf16[1,1,128,2048]{3,2,1,0:T(8,128)(2,1)S(1)}, bf16[1,1,128,2048]{3,2,1,0:T(8,128)(2,1)}, u32[]{:S(2)}) copy-start(bf16[1,1,128,2048]{3,2,1,0:T(8,128)(2,1)} %fusion.4) | copy-start | bytes 1572868
  121.4 8.8 %collective-permute-start.16 = (bf16[1,64,2048]{2,1,0:T(8,128)(2,1)}, bf16[1,64,2048]{2,1,0:T(8,128)(2,1)S(1)}, u32[]{:S(2)}, u32[]{:S(2)}) collective-permute-start(bf16[1,64,2048]{2,1,0:T(8,128)(2,1)} %collective-permute-done.14), channel_id=1, source_target_pairs={{30,0},{0,2},{2,4},{4,6},{6,8},{8,10},{10,12},{12,14},{14,16},{16,... | collective-permute-start | bytes 786440 | tf_op jit(solution)/shard_map/ppermute | solution.py:16
  122.9 8.6 %collective-permute-start.2 = (bf16[1,64,2048]{2,1,0:T(8,128)(2,1)}, bf16[1,64,2048]{2,1,0:T(8,128)(2,1)S(1)}, u32[]{:S(2)}, u32[]{:S(2)}) collective-permute-start(bf16[1,64,2048]{2,1,0:T(8,128)(2,1)} %collective-permute-done.1), channel_id=1, source_target_pairs={{2,0},{4,2},{6,4},{8,6},{10,8},{12,10},{14,12},{16,14},{18,16},{20... | collective-permute-start | bytes 786440 | tf_op jit(solution)/shard_map/ppermute | solution.py:16
  134.0 9.5 %copy-start.6 = (f32[1,1,1,4096]{3,2,1,0:T(1,128)S(1)}, f32[1,1,1,4096]{3,2,1,0:T(1,128)}, u32[]{:S(2)}) copy-start(f32[1,1,1,4096]{3,2,1,0:T(1,128)} %mul.668) | copy-start | bytes 49156
  134.2 9.5 %copy-start.5 = (f32[1,1,1,4096]{3,2,1,0:T(1,128)S(1)}, f32[1,1,1,4096]{3,2,1,0:T(1,128)}, u32[]{:S(2)}) copy-start(f32[1,1,1,4096]{3,2,1,0:T(1,128)} %mul.738) | copy-start | bytes 49156
  163.6 45.8 %copy-start.1 = (bf16[576,2048]{1,0:T(8,128)(2,1)S(1)}, bf16[576,2048]{1,0:T(8,128)(2,1)}, u32[]{:S(2)}) copy-start(bf16[576,2048]{1,0:T(8,128)(2,1)} %param.7) | copy-start | bytes 7077892
Sparse Core Ops, SparseCore 0:
  163.7 33.0 reduce-scatter.3
where the time goes:
time: 217 us; the launch traced here: 216 us
  matrix products  52.1 us (24%)
  waiting for transfers between devices  47.1 us (22%)
  starting transfers between devices  42.1 us (19%)
  local copies, waits for them, and re-layouts  37.9 us (17%)
  between operations  26.2 us (12%)
  other arithmetic  5.69 us (3%)
  blocking collectives  5.15 us (2%)
    dot_general x8, matrix products, project(): jnp.dot(flattened, interp_vectors, preferred_element_type=jnp.float32)  36.9 us
    ppermute x18, starting transfers between devices, from_behind(): return lax.ppermute(block, axis, route)  35 us
    unnamed x2, waiting for transfers between devices  33.2 us
    unnamed x26, local copies, waits for them, and re-layouts  31.7 us
    dot_general x7, matrix products, pair_block(): jnp.einsum('klxg,klyg->klxy', weighted, pair_waves[:, :, NC * NC:], prefe...  9.15 us
    ppermute x18, waiting for transfers between devices, from_behind(): return lax.ppermute(block, axis, route)  8.04 us
    all_to_all x1, waiting for transfers between devices, per_device(): lax.all_to_all(queries, 'ka', split_axis=0, concat_axis=0, tiled=True)  5.87 us
    dot_general x7, matrix products, pair_block(): jnp.einsum('kxg,lyg->klxy', weighted_x, partner_ex, preferred_element_typ...  5.45 us
  transfers between devices with their start and end apart: 21, of which 5 were waited for; matrix products, arithmetic and copies ran while one was open for 24% of the time, Pallas kernels for 0%

commit v1 on v0

v1 whole, which is shorter than its diff:
```python
import functools

import jax
import jax.numpy as jnp
from jax import lax
from jax.experimental import pallas as pl
from jax.experimental.pallas import tpu as pltpu
from jax.sharding import PartitionSpec as P

NV = 8
NC = 8
NG = 4096
NKX = 96
RSTEPS = 3
NP = NV * NC
TILE = 256
F32, BF16, I32 = jnp.float32, jnp.bfloat16, jnp.int32


def dot(a, b):
    return lax.dot_general(a, b, (((1,), (0,)), ((), ())), preferred_element_type=F32)


def dot_t(a, b):
    return lax.dot_general(a, b, (((1,), (1,)), ((), ())), preferred_element_type=F32)


def iota(shape, dim):
    return lax.broadcasted_iota(I32, shape, dim)


def flip(x, j, bits):
    for s in range(bits):
        if (j >> s) & 1:
            x = x + (1 << s) - 2 * (1 << s) * ((x // (1 << s)) % 2)
    return x


def reverse(i, bits):
    return sum(((i >> s) & 1) << (bits - 1 - s) for s in range(bits))


def onehot(cond):
    return jnp.where(cond, 1.0, 0.0).astype(BF16)


def kernel(
    n_ka, n_ga,
    orb, kpt, bare, interp, screening, out,
    slots, kall, table, pick, arrived, points, weights, waves, sbuf, rbuf,
    osend, orecv, ksend, krecv, tsem, isem, psend, precv, fsend, frecv,
):
    k, g = lax.axis_index("ka"), lax.axis_index("ga")
    bits = n_ka.bit_length() - 1
    steps = RSTEPS + 1
    half_pts = orb.shape[2]
    pts, cols = interp.shape
    tiles = cols // TILE
    rows_here = screening.shape[0]
    share = sbuf.shape[1] // n_ga

    def ka(x):
        return lax.rem(x + n_ka, n_ka)

    def ga(x):
        return lax.rem(x + n_ga, n_ga)

    def remote(src, dst, ss, rs, kk, gg):
        return pltpu.make_async_remote_copy(
            src_ref=src, dst_ref=dst, send_sem=ss, recv_sem=rs,
            device_id=(kk, gg), device_id_type=pl.DeviceIdType.MESH,
        )

    def load_tile(t):
        at = pl.ds(pl.multiple_of(t * TILE, TILE), TILE)
        return pltpu.make_async_copy(interp.at[:, at], weights.at[t], isem.at[t])

    barrier = pltpu.get_barrier_semaphore()
    peers = [(flip(k, j, bits), g) for j in range(1, n_ka)]
    peers += [(ka(k + d), ga(g + j)) for d in range(-RSTEPS, RSTEPS + 1) for j in range(1, n_ga)]
    for kk, gg in peers:
        pl.semaphore_signal(barrier, inc=1, device_id=(kk, gg), device_id_type=pl.DeviceIdType.MESH)
    table_copy = pltpu.make_async_copy(screening, table, tsem.at[0])
    table_copy.start()
    for t in range(tiles):
        load_tile(t).start()
    point = kpt[0]
    kall[k, 0] = jnp.full((8, 128), point // NKX, I32)
    kall[k, 1] = jnp.full((8, 128), point % NKX, I32)
    slots[0, g] = orb[0]
    pl.semaphore_wait(barrier, len(peers))

    def kpt_copy(j, owner):
        return remote(kall.at[owner], kall.at[owner], ksend.at[j], krecv.at[j], flip(k, j, bits), g)

    for j in range(1, n_ka):
        kpt_copy(j, k).start()
    moves = [(d, j) for d in range(steps) for j in range(n_ga) if d or j]

    def orb_copy(d, j, gg):
        return remote(
            orb.at[0], slots.at[d, gg], osend.at[d, j], orecv.at[d, j], ka(k + d), ga(g + j)
        )

    for d, j in moves:
        orb_copy(d, j, g).start()

    for j in range(1, n_ka):
        kpt_copy(j, flip(k, j, bits)).wait_recv()

    table_copy.wait()
    sub = iota((8, 128), 0)
    lane = iota((16, rows_here), 1)
    pieces = []
    for i in range(n_ka):
        dest = flip(k, reverse(i, bits), bits)
        dx, dy = kall[dest, 0], kall[dest, 1]
        want = jnp.zeros((8, 128), I32)
        for d in range(1, steps):
            other = ka(dest - d)
            x, y = dx - kall[other, 0], dy - kall[other, 1]
            there = jnp.where(x < 0, x + NKX, x) * NKX + jnp.where(y < 0, y + NKX, y)
            back = jnp.where(x > 0, NKX - x, -x) * NKX + jnp.where(y > 0, NKX - y, -y)
            want = jnp.where(sub == 2 * d - 1, there, want)
            want = jnp.where(sub == 2 * d, back, want)
        local = (want - k * rows_here)[:, :1]
        local = jnp.concatenate([local, local], axis=0)
        pieces.append(jnp.where(lane == local, 1.0, 0.0))
    picker = jnp.concatenate(pieces, axis=0).astype(BF16)
    half_cols = cols // 2
    picked = dot(picker, table[...])
    upper = (iota((n_ka * 16, half_cols), 0) // 8) % 2
    picked = jnp.where(upper == 0, picked[:, :half_cols], picked[:, half_cols:])
    pick[...] = picked.astype(BF16).reshape(n_ka, 16, half_cols)

    def pick_copy(s):
        half = n_ka >> (s + 1)
        return remote(
            pick.at[pl.ds(half, half)], arrived.at[pl.ds(half, half)],
            psend.at[s], precv.at[s], flip(k, 1 << s, bits), g,
        )

    def pick_step(s):
        half = n_ka >> (s + 1)
        pick_copy(s).wait_recv()
        pick[:half] = (pick[:half].astype(F32) + arrived[half:2 * half].astype(F32)).astype(BF16)
        if s + 1 < bits:
            pick_copy(s + 1).start()

    pick_copy(0).start()

    width = 512
    for d in range(steps):
        for j in range(n_ga):
            if d or j:
                orb_copy(d, j, ga(g - j)).wait_recv()

        def products(c, carry, d=d):
            h, off = c // (half_pts // width), c % (half_pts // width)
            at = pl.ds(pl.multiple_of(off * width, width), width)
            to = pl.ds(pl.multiple_of(c * width, width), width)
            own = slots[0, h, :, at].astype(F32)
            par = slots[d, h, :, at].astype(F32)
            own_v, own_c, par_v, par_c = own[:NV], own[NV:], par[:NV], par[NV:]
            ex = jnp.concatenate([par_v[i:i + 1] * par_c for i in range(NV)], axis=0)
            cond = jnp.concatenate([own_c[i:i + 1] * par_c for i in range(NC)], axis=0)
            vale = jnp.concatenate([par_v[i:i + 1] * own_v for i in range(NV)], axis=0)
            points[pl.ds(d * NP, NP), to] = ex.astype(BF16)
            points[pl.ds((steps + 2 * d) * NP, NP), to] = cond.astype(BF16)
            points[pl.ds((steps + 2 * d + 1) * NP, NP), to] = vale.astype(BF16)
            return carry

        lax.fori_loop(0, pts // width, products, 0)

    inside = min(bits, tiles - 1)

    def project(t, carry):
        for s in range(inside):
            @pl.when(t == s + 1)
            def _(s=s):
                pick_step(s)
        load_tile(t).wait()
        at = pl.ds(pl.multiple_of(t * TILE, TILE), TILE)
        waves[:, at] = dot(points[...], weights[t]).astype(BF16)
        return carry

    lax.fori_loop(0, tiles, project, 0)
    for s in range(inside, bits):
        pick_step(s)

    screen = pick[0].astype(F32)
    screen = jnp.concatenate([screen[:8], screen[8:]], axis=1)
    weighted_x = (waves[:NP].astype(F32) * bare[...]).astype(BF16)
    ex_t = dot_t(waves[:steps * NP], weighted_x)

    quarter = sbuf.shape[1]
    rep_rows = NV * quarter
    r, c = iota((rep_rows, NP), 0), iota((rep_rows, NP), 1)
    r_v2, r_v, r_ch = r // quarter, (r % quarter) // 4, r % 4
    rep_own, rep_mir = onehot(c == r_v2 * NV + r_v), onehot(c == r_v * NV + r_v2)
    keep_own, keep_mir = (c // 8) // 2 == r_ch, (c % 8) // 2 == r_ch
    r, c = iota((NP, 128), 0), iota((NP, 128), 1)
    c_cl, c_v2, c_c2 = c // 64, (c % 64) // 8, c % 8
    fit_own = ((r // 8) % 2 == c_cl) & (r % 8 == c_c2)
    fit_mir = (r % 2 == c_cl) & (r // 8 == c_c2)
    place = [onehot(c == r + 64 * cl) for cl in range(2)]
    r, c = iota((quarter, NP), 0), iota((quarter, NP), 1)
    rows_of = [onehot(c == (r // 4) * 8 + (r % 4) * 2 + cl) for cl in range(2)]

    own_x, mir_x = [], []
    for d in range(steps):
        base = (steps + 2 * d) * NP
        cond = waves[base:base + NP].astype(F32)
        vale = waves[base + NP:base + 2 * NP]
        row = max(2 * d - 1, 0)
        term = dot_t(vale, (cond * screen[row:row + 1]).astype(BF16)).astype(BF16)
        own_x.append(jnp.where(keep_own, dot(rep_own, term), 0.0).astype(BF16))
        if d:
            term = dot_t(vale, (cond * screen[2 * d:2 * d + 1]).astype(BF16)).astype(BF16)
            mir_x.append(jnp.where(keep_mir, dot(rep_mir, term), 0.0).astype(BF16))

    def gathered(parts, fit):
        total = 0.0
        for v2 in range(NV):
            stacked = jnp.concatenate([x[v2 * quarter:(v2 + 1) * quarter] for x in parts], axis=0)
            total = total + dot(stacked, onehot(fit & (c_v2 == v2)))
        return total

    direct = [gathered(own_x, fit_own), gathered(mir_x, fit_mir)]
    for e in range(2 * RSTEPS + 1):
        d = e if e < steps else e - RSTEPS
        exch = ex_t[d * NP:(d + 1) * NP].astype(BF16)
        pick_rows = dot_t if e < steps else dot
        spread = sum(dot(pick_rows(rows_of[cl], exch).astype(BF16), place[cl]) for cl in range(2))
        at = (e if e < steps else e - steps) * quarter
        sbuf[e] = 2.0 * spread - direct[e // steps][at:at + quarter]

    def own_rows(gg):
        return pl.ds(pl.multiple_of(gg * share, share), share)

    def final_copy(d, j, gg):
        to = ga(g + j)
        entries = pl.ds(RSTEPS + d, 1) if d else pl.ds(0, steps)
        return remote(
            sbuf.at[entries, own_rows(to)], rbuf.at[gg, entries],
            fsend.at[d, j], frecv.at[d, j], ka(k - d), to,
        )

    for d, j in moves:
        final_copy(d, j, g).start()
    for d, j in moves:
        final_copy(d, j, ga(g - j)).wait_recv()
    scale = NG ** (-0.5)
    for d in range(steps):
        total = sbuf[d, own_rows(g)]
        for j in range(1, n_ga):
            total = total + rbuf[ga(g - j), d]
        out[pl.ds((RSTEPS + d) * share, share)] = total * scale
        if d:
            total = rbuf[g, RSTEPS + d]
            for j in range(1, n_ga):
                total = total + rbuf[ga(g - j), RSTEPS + d]
            out[pl.ds((RSTEPS - d) * share, share)] = total * scale

    for d, j in moves:
        final_copy(d, j, g).wait_send()
        orb_copy(d, j, g).wait_send()
    for j in range(1, n_ka):
        kpt_copy(j, k).wait_send()
    for s in range(bits):
        pick_copy(s).wait_send()


def per_device(n_ka, n_ga, orbitals, interp_vectors, screening, bare_coulomb, slab_kpoints):
    _, bands, half_pts = orbitals.shape
    pts, cols = interp_vectors.shape
    steps = RSTEPS + 1
    entries = 2 * RSTEPS + 1
    rows = 3 * steps * NP
    quarter = NP * NP // 128
    share = quarter // n_ga
    tiles = cols // TILE
    bits = n_ka.bit_length() - 1
    dma = pltpu.SemaphoreType.DMA
    vmem = pl.BlockSpec(memory_space=pltpu.VMEM)
    hbm = pl.BlockSpec(memory_space=pl.ANY)
    result = pl.pallas_call(
        functools.partial(kernel, n_ka, n_ga),
        out_shape=jax.ShapeDtypeStruct((entries * share, 128), F32),
        in_specs=[vmem, pl.BlockSpec(memory_space=pltpu.SMEM), vmem, hbm, hbm],
        out_specs=vmem,
        scratch_shapes=[
            pltpu.VMEM((steps, n_ga, bands, half_pts), BF16),
            pltpu.VMEM((n_ka, 2, 8, 128), I32),
            pltpu.VMEM(screening.shape, BF16),
            pltpu.VMEM((n_ka, 16, cols // 2), BF16),
            pltpu.VMEM((n_ka, 16, cols // 2), BF16),
            pltpu.VMEM((rows, pts), BF16),
            pltpu.VMEM((tiles, pts, TILE), BF16),
            pltpu.VMEM((rows, cols), BF16),
            pltpu.VMEM((entries, quarter, 128), F32),
            pltpu.VMEM((n_ga, entries, share, 128), F32),
            dma((steps, n_ga)), dma((steps, n_ga)),
            dma((n_ka,)), dma((n_ka,)),
            dma((1,)), dma((tiles,)),
            dma((bits,)), dma((bits,)),
            dma((steps, n_ga)), dma((steps, n_ga)),
        ],
        compiler_params=pltpu.CompilerParams(
            collective_id=0, has_side_effects=True, vmem_limit_bytes=56 * 2 ** 20
        ),
        cost_estimate=pl.CostEstimate(
            flops=2 * rows * pts * cols, bytes_accessed=2 * pts * cols, transcendentals=0
        ),
    )(orbitals, slab_kpoints, bare_coulomb.reshape(1, -1), interp_vectors, screening)
    return result.reshape(1, entries, 1, share * 128)


def solution(mesh):
    in_specs = (P("ka", None, "ga"), P(None, "ga"), P("ka", "ga"), P("ga"), P("ka"))
    out_specs = P("ka", None, None, "ga")
    return jax.shard_map(
        functools.partial(per_device, mesh.shape["ka"], mesh.shape["ga"]),
        mesh=mesh, in_specs=in_specs, out_specs=out_specs, check_vma=False,
    )
```

time: 217 us -> 50.4 us (0.23)
  matrix products: 52.1 us -> 0 us
  Pallas kernels: 0 us -> 48.1 us
  waiting for transfers between devices: 47.1 us -> 0 us
  starting transfers between devices: 42.1 us -> 0 us
  local copies, waits for them, and re-layouts: 37.9 us -> 1.45 us
  between operations: 26.2 us -> 0.66 us
  other arithmetic: 5.69 us -> 0 us
  blocking collectives: 5.15 us -> 0 us
    dot_general x23 -> x0, matrix products: 52.1 us -> none  [the longest x8 36.9 us: project(): jnp.dot(flattened, interp_vectors, preferred_element_type=jnp.float32)]
    pallas_call x0 -> x1, Pallas kernels: none -> 48.1 us  [per_device(): pl.pallas_call(functools.partial(kernel, n_ka, n_ga), out_shape=jax.Shape...]
    ppermute x18 -> x0, starting transfers between devices: 35 us -> none  [from_behind(): return lax.ppermute(block, axis, route)]
    unnamed x2 -> x0, waiting for transfers between devices: 33.2 us -> none
    unnamed x26 -> x1, local copies, waits for them, and re-layouts: 31.7 us -> 1.45 us
    ppermute x18 -> x0, waiting for transfers between devices: 8.04 us -> none  [from_behind(): return lax.ppermute(block, axis, route)]
    all_to_all x2 -> x0, starting transfers between devices: 7.04 us -> none  [the longest x1 3.57 us: per_device(): lax.all_to_all(replies, 'ka', split_axis=0, concat_axis=0, tiled=True)]
    all_to_all x2 -> x0, waiting for transfers between devices: 5.88 us -> none  [the longest x1 5.87 us: per_device(): lax.all_to_all(queries, 'ka', split_axis=0, concat_axis=0, tiled=True)]
  transfers between devices with their start and end apart: 21 -> 0, of which waited for: 5 -> 0; matrix products, arithmetic and copies ran while one was open for 24% -> 0% of each run, Pallas kernels for 0% -> 0%
where the time goes in v1:
time: 50.4 us; the launch traced here: 50.2 us
  Pallas kernels  48.1 us (95%)
  local copies, waits for them, and re-layouts  1.45 us (3%)
  between operations  0.66 us (1%)
    pallas_call x1, Pallas kernels, per_device(): pl.pallas_call(functools.partial(kernel, n_ka, n_ga), out_shape=jax.Shape...  48.1 us
    unnamed x1, local copies, waits for them, and re-layouts  1.45 us

profile of v1, /device:TPU:0, one launch (start us, length us, event | category | flops | bytes accessed | tf_op | source)
XLA Modules:
  0.0 50.2 jit_solution(3438319191809310415)
XLA Ops:
  0.7 48.1 %shard_map.55 = f32[112,128]{1,0:T(8,128)} custom-call(bf16[1,16,2048]{2,1,0:T(8,128)(2,1)} %orb.1, s32[1]{0:T(128)S(6)} %copy.9.kpt, f32[1,2048]{1,0:T(1,128)} %bitcast.3, bf16[4096,2048]{1,0:T(8,128)(2,1)} %interp.1, bf16[576,2048]{1,0:T(8,128)(2,1)} %screening.1), custom_call_target="tpu_custom_call" | custom-call | flops 12884901888 | bytes 16777216 | tf_op jit(solution)/shard_map/pallas_call | solution.py:287
  48.7 1.4 %copy.10 = f32[1,7,1,2048]{3,2,1,0:T(1,128)} copy(f32[1,7,1,2048]{3,2,1,0:T(1,128)} %bitcast.2) | data formatting | bytes 114688

commit v2 on v1

--- a/solution.py
+++ b/solution.py
@@ -27,13 +27,6 @@
 
 def iota(shape, dim):
     return lax.broadcasted_iota(I32, shape, dim)
-
-
-def flip(x, j, bits):
-    for s in range(bits):
-        if (j >> s) & 1:
-            x = x + (1 << s) - 2 * (1 << s) * ((x // (1 << s)) % 2)
-    return x
 
 
 def reverse(i, bits):
@@ -59,6 +52,9 @@
     rows_here = screening.shape[0]
     share = sbuf.shape[1] // n_ga
 
+    swaps = [(1 << s) * (1 - 2 * lax.rem(lax.div(k, 1 << s), 2)) for s in range(bits)]
+    flips = [sum([swaps[s] for s in range(bits) if (j >> s) & 1], k) for j in range(n_ka)]
+
     def ka(x):
         return lax.rem(x + n_ka, n_ka)
 
@@ -76,7 +72,7 @@
         return pltpu.make_async_copy(interp.at[:, at], weights.at[t], isem.at[t])
 
     barrier = pltpu.get_barrier_semaphore()
-    peers = [(flip(k, j, bits), g) for j in range(1, n_ka)]
+    peers = [(flips[j], g) for j in range(1, n_ka)]
     peers += [(ka(k + d), ga(g + j)) for d in range(-RSTEPS, RSTEPS + 1) for j in range(1, n_ga)]
     for kk, gg in peers:
         pl.semaphore_signal(barrier, inc=1, device_id=(kk, gg), device_id_type=pl.DeviceIdType.MESH)
@@ -85,16 +81,14 @@
     for t in range(tiles):
         load_tile(t).start()
     point = kpt[0]
-    kall[k, 0] = jnp.full((8, 128), point // NKX, I32)
-    kall[k, 1] = jnp.full((8, 128), point % NKX, I32)
+    kall[k, 0:1] = jnp.full((1, 128), lax.div(point, NKX), I32)
+    kall[k, 1:2] = jnp.full((1, 128), lax.rem(point, NKX), I32)
     slots[0, g] = orb[0]
     pl.semaphore_wait(barrier, len(peers))
 
     def kpt_copy(j, owner):
-        return remote(kall.at[owner], kall.at[owner], ksend.at[j], krecv.at[j], flip(k, j, bits), g)
-
-    for j in range(1, n_ka):
-        kpt_copy(j, k).start()
+        return remote(kall.at[owner], kall.at[owner], ksend.at[j], krecv.at[j], flips[j], g)
+
     moves = [(d, j) for d in range(steps) for j in range(n_ga) if d or j]
 
     def orb_copy(d, j, gg):
@@ -102,23 +96,69 @@
             orb.at[0], slots.at[d, gg], osend.at[d, j], orecv.at[d, j], ka(k + d), ga(g + j)
         )
 
-    for d, j in moves:
+    head = [m for m in moves if m[0] == 0]
+    for d, j in head:
         orb_copy(d, j, g).start()
-
     for j in range(1, n_ka):
-        kpt_copy(j, flip(k, j, bits)).wait_recv()
+        kpt_copy(j, k).start()
+    for d, j in moves[len(head):]:
+        orb_copy(d, j, g).start()
+
+    first = 3 * NP
+
+    def ex_at(d):
+        return first + (d - 1) * NP if d else 0
+
+    def pair_at(d):
+        return first + RSTEPS * NP + (d - 1) * 2 * NP if d else NP
+
+    width = 512
+
+    def products_of(d):
+        for j in range(n_ga):
+            if d or j:
+                orb_copy(d, j, ga(g - j)).wait_recv()
+
+        def products(c, carry):
+            h, off = lax.div(c, half_pts // width), lax.rem(c, half_pts // width)
+            at = pl.ds(pl.multiple_of(off * width, width), width)
+            to = pl.ds(pl.multiple_of(c * width, width), width)
+            own = slots[0, h, :, at].astype(F32)
+            par = slots[d, h, :, at].astype(F32)
+            own_v, own_c, par_v, par_c = own[:NV], own[NV:], par[:NV], par[NV:]
+            ex = jnp.concatenate([par_v[i:i + 1] * par_c for i in range(NV)], axis=0)
+            cond = jnp.concatenate([own_c[i:i + 1] * par_c for i in range(NC)], axis=0)
+            vale = jnp.concatenate([par_v[i:i + 1] * own_v for i in range(NV)], axis=0)
+            points[pl.ds(ex_at(d), NP), to] = ex.astype(BF16)
+            points[pl.ds(pair_at(d), NP), to] = cond.astype(BF16)
+            points[pl.ds(pair_at(d) + NP, NP), to] = vale.astype(BF16)
+            return carry
+
+        lax.fori_loop(0, pts // width, products, 0)
+
+    def project_head(t, carry):
+        load_tile(t).wait()
+        at = pl.ds(pl.multiple_of(t * TILE, TILE), TILE)
+        waves[:first, at] = dot(points[:first], weights[t]).astype(BF16)
+        return carry
+
+    products_of(0)
+    lax.fori_loop(0, tiles, project_head, 0)
+
+    for j in range(1, n_ka):
+        kpt_copy(j, flips[j]).wait_recv()
 
     table_copy.wait()
     sub = iota((8, 128), 0)
     lane = iota((16, rows_here), 1)
     pieces = []
     for i in range(n_ka):
-        dest = flip(k, reverse(i, bits), bits)
-        dx, dy = kall[dest, 0], kall[dest, 1]
+        dest = flips[reverse(i, bits)]
+        dx, dy = kall[dest, 0:1], kall[dest, 1:2]
         want = jnp.zeros((8, 128), I32)
         for d in range(1, steps):
             other = ka(dest - d)
-            x, y = dx - kall[other, 0], dy - kall[other, 1]
+            x, y = dx - kall[other, 0:1], dy - kall[other, 1:2]
             there = jnp.where(x < 0, x + NKX, x) * NKX + jnp.where(y < 0, y + NKX, y)
             back = jnp.where(x > 0, NKX - x, -x) * NKX + jnp.where(y > 0, NKX - y, -y)
             want = jnp.where(sub == 2 * d - 1, there, want)
@@ -129,7 +169,7 @@
     picker = jnp.concatenate(pieces, axis=0).astype(BF16)
     half_cols = cols // 2
     picked = dot(picker, table[...])
-    upper = (iota((n_ka * 16, half_cols), 0) // 8) % 2
+    upper = iota((n_ka * 16, half_cols), 0) & 8
     picked = jnp.where(upper == 0, picked[:, :half_cols], picked[:, half_cols:])
     pick[...] = picked.astype(BF16).reshape(n_ka, 16, half_cols)
 
@@ -137,7 +177,7 @@
         half = n_ka >> (s + 1)
         return remote(
             pick.at[pl.ds(half, half)], arrived.at[pl.ds(half, half)],
-            psend.at[s], precv.at[s], flip(k, 1 << s, bits), g,
+            psend.at[s], precv.at[s], flips[1 << s], g,
         )
 
     def pick_step(s):
@@ -149,28 +189,8 @@
 
     pick_copy(0).start()
 
-    width = 512
-    for d in range(steps):
-        for j in range(n_ga):
-            if d or j:
-                orb_copy(d, j, ga(g - j)).wait_recv()
-
-        def products(c, carry, d=d):
-            h, off = c // (half_pts // width), c % (half_pts // width)
-            at = pl.ds(pl.multiple_of(off * width, width), width)
-            to = pl.ds(pl.multiple_of(c * width, width), width)
-            own = slots[0, h, :, at].astype(F32)
-            par = slots[d, h, :, at].astype(F32)
-            own_v, own_c, par_v, par_c = own[:NV], own[NV:], par[:NV], par[NV:]
-            ex = jnp.concatenate([par_v[i:i + 1] * par_c for i in range(NV)], axis=0)
-            cond = jnp.concatenate([own_c[i:i + 1] * par_c for i in range(NC)], axis=0)
-            vale = jnp.concatenate([par_v[i:i + 1] * own_v for i in range(NV)], axis=0)
-            points[pl.ds(d * NP, NP), to] = ex.astype(BF16)
-            points[pl.ds((steps + 2 * d) * NP, NP), to] = cond.astype(BF16)
-            points[pl.ds((steps + 2 * d + 1) * NP, NP), to] = vale.astype(BF16)
-            return carry
-
-        lax.fori_loop(0, pts // width, products, 0)
+    for d in range(1, steps):
+        products_of(d)
 
     inside = min(bits, tiles - 1)
 
@@ -179,9 +199,8 @@
             @pl.when(t == s + 1)
             def _(s=s):
                 pick_step(s)
-        load_tile(t).wait()
         at = pl.ds(pl.multiple_of(t * TILE, TILE), TILE)
-        waves[:, at] = dot(points[...], weights[t]).astype(BF16)
+        waves[first:, at] = dot(points[first:], weights[t]).astype(BF16)
         return carry
 
     lax.fori_loop(0, tiles, project, 0)
@@ -191,25 +210,25 @@
     screen = pick[0].astype(F32)
     screen = jnp.concatenate([screen[:8], screen[8:]], axis=1)
     weighted_x = (waves[:NP].astype(F32) * bare[...]).astype(BF16)
-    ex_t = dot_t(waves[:steps * NP], weighted_x)
+    ex_t = [dot_t(waves[ex_at(d):ex_at(d) + NP], weighted_x).astype(BF16) for d in range(steps)]
 
     quarter = sbuf.shape[1]
     rep_rows = NV * quarter
     r, c = iota((rep_rows, NP), 0), iota((rep_rows, NP), 1)
-    r_v2, r_v, r_ch = r // quarter, (r % quarter) // 4, r % 4
+    r_v2, r_v, r_ch = r >> (quarter.bit_length() - 1), (r & (quarter - 1)) >> 2, r & 3
     rep_own, rep_mir = onehot(c == r_v2 * NV + r_v), onehot(c == r_v * NV + r_v2)
-    keep_own, keep_mir = (c // 8) // 2 == r_ch, (c % 8) // 2 == r_ch
+    keep_own, keep_mir = c >> 4 == r_ch, (c & 7) >> 1 == r_ch
     r, c = iota((NP, 128), 0), iota((NP, 128), 1)
-    c_cl, c_v2, c_c2 = c // 64, (c % 64) // 8, c % 8
-    fit_own = ((r // 8) % 2 == c_cl) & (r % 8 == c_c2)
-    fit_mir = (r % 2 == c_cl) & (r // 8 == c_c2)
+    c_cl, c_v2, c_c2 = c >> 6, (c & 63) >> 3, c & 7
+    fit_own = ((r >> 3) & 1 == c_cl) & (r & 7 == c_c2)
+    fit_mir = (r & 1 == c_cl) & (r >> 3 == c_c2)
     place = [onehot(c == r + 64 * cl) for cl in range(2)]
     r, c = iota((quarter, NP), 0), iota((quarter, NP), 1)
-    rows_of = [onehot(c == (r // 4) * 8 + (r % 4) * 2 + cl) for cl in range(2)]
+    rows_of = [onehot(c == (r >> 2) * 8 + (r & 3) * 2 + cl) for cl in range(2)]
 
     own_x, mir_x = [], []
     for d in range(steps):
-        base = (steps + 2 * d) * NP
+        base = pair_at(d)
         cond = waves[base:base + NP].astype(F32)
         vale = waves[base + NP:base + 2 * NP]
         row = max(2 * d - 1, 0)
@@ -229,7 +248,7 @@
     direct = [gathered(own_x, fit_own), gathered(mir_x, fit_mir)]
     for e in range(2 * RSTEPS + 1):
         d = e if e < steps else e - RSTEPS
-        exch = ex_t[d * NP:(d + 1) * NP].astype(BF16)
+        exch = ex_t[d]
         pick_rows = dot_t if e < steps else dot
         spread = sum(dot(pick_rows(rows_of[cl], exch).astype(BF16), place[cl]) for cl in range(2))
         at = (e if e < steps else e - steps) * quarter
@@ -291,7 +310,7 @@
         out_specs=vmem,
         scratch_shapes=[
             pltpu.VMEM((steps, n_ga, bands, half_pts), BF16),
-            pltpu.VMEM((n_ka, 2, 8, 128), I32),
+            pltpu.VMEM((n_ka, 2, 128), I32),
             pltpu.VMEM(screening.shape, BF16),
             pltpu.VMEM((n_ka, 16, cols // 2), BF16),
             pltpu.VMEM((n_ka, 16, cols // 2), BF16),

time: 50.4 us -> 46.4 us (0.921)
  Pallas kernels: 48.1 us -> 44.1 us
    pallas_call x1, Pallas kernels: 48.1 us -> 44.1 us  [per_device(): pl.pallas_call(functools.partial(kernel, n_ka, n_ga), out_shape=jax.Shape...]
where the time goes in v2:
time: 46.4 us; the launch traced here: 46.2 us
  Pallas kernels  44.1 us (95%)
  local copies, waits for them, and re-layouts  1.45 us (3%)
  between operations  0.66 us (1%)
    pallas_call x1, Pallas kernels, per_device(): pl.pallas_call(functools.partial(kernel, n_ka, n_ga), out_shape=jax.Shape...  44.1 us
    unnamed x1, local copies, waits for them, and re-layouts  1.45 us

profile of v2, /device:TPU:0, one launch (start us, length us, event | category | flops | bytes accessed | tf_op | source)
XLA Modules:
  0.0 46.2 jit_solution(13284457170478115013)
XLA Ops:
  0.7 44.1 %shard_map.55 = f32[112,128]{1,0:T(8,128)} custom-call(bf16[1,16,2048]{2,1,0:T(8,128)(2,1)} %orb.1, s32[1]{0:T(128)S(6)} %copy.9.kpt, f32[1,2048]{1,0:T(1,128)} %bitcast.3, bf16[4096,2048]{1,0:T(8,128)(2,1)} %interp.1, bf16[576,2048]{1,0:T(8,128)(2,1)} %screening.1), custom_call_target="tpu_custom_call" | custom-call | flops 12884901888 | bytes 16777216 | tf_op jit(solution)/shard_map/pallas_call | solution.py:306
  44.8 1.4 %copy.10 = f32[1,7,1,2048]{3,2,1,0:T(1,128)} copy(f32[1,7,1,2048]{3,2,1,0:T(1,128)} %bitcast.2) | data formatting | bytes 114688

commit v3 on v2

--- a/solution.py
+++ b/solution.py
@@ -13,7 +13,7 @@
 NKX = 96
 RSTEPS = 3
 NP = NV * NC
-TILE = 256
+TILE = 512
 F32, BF16, I32 = jnp.float32, jnp.bfloat16, jnp.int32
 
 
@@ -192,11 +192,11 @@
     for d in range(1, steps):
         products_of(d)
 
-    inside = min(bits, tiles - 1)
+    inside = min(bits, tiles)
 
     def project(t, carry):
         for s in range(inside):
-            @pl.when(t == s + 1)
+            @pl.when(t == s)
             def _(s=s):
                 pick_step(s)
         at = pl.ds(pl.multiple_of(t * TILE, TILE), TILE)

time: 46.4 us -> 42.7 us (0.920)
  Pallas kernels: 44.1 us -> 40.4 us
    pallas_call x1, Pallas kernels: 44.1 us -> 40.4 us  [per_device(): pl.pallas_call(functools.partial(kernel, n_ka, n_ga), out_shape=jax.Shape...]
where the time goes in v3:
time: 42.7 us; the launch traced here: 42.5 us
  Pallas kernels  40.4 us (95%)
  local copies, waits for them, and re-layouts  1.45 us (3%)
  between operations  0.66 us (2%)
    pallas_call x1, Pallas kernels, per_device(): pl.pallas_call(functools.partial(kernel, n_ka, n_ga), out_shape=jax.Shape...  40.4 us
    unnamed x1, local copies, waits for them, and re-layouts  1.45 us

profile of v3, /device:TPU:0, one launch (start us, length us, event | category | flops | bytes accessed | tf_op | source)
XLA Modules:
  0.0 42.5 jit_solution(116106471051307332)
XLA Ops:
  0.7 40.4 %shard_map.55 = f32[112,128]{1,0:T(8,128)} custom-call(bf16[1,16,2048]{2,1,0:T(8,128)(2,1)} %orb.1, s32[1]{0:T(128)S(6)} %copy.9.kpt, f32[1,2048]{1,0:T(1,128)} %bitcast.3, bf16[4096,2048]{1,0:T(8,128)(2,1)} %interp.1, bf16[576,2048]{1,0:T(8,128)(2,1)} %screening.1), custom_call_target="tpu_custom_call" | custom-call | flops 12884901888 | bytes 16777216 | tf_op jit(solution)/shard_map/pallas_call | solution.py:306
  41.0 1.4 %copy.10 = f32[1,7,1,2048]{3,2,1,0:T(1,128)} copy(f32[1,7,1,2048]{3,2,1,0:T(1,128)} %bitcast.2) | data formatting | bytes 114688
